TPU v7x, 32 devices: a whole 2x2x4 slice. The times are simulated.
32 devices in a mesh: dp: 8 (over z, x), tensor: 4 (over y, core).
Axes of the slice: x: 2, y: 2, z: 4, core: 2. Of those that a mesh axis runs over, the one named last changes fastest.
Arguments:
- tokens: bfloat16 [10976, 1280], P(('dp', 'tensor')), may hold values from -6 to 6
- grad_out: bfloat16 [10976, 1280], P(('dp', 'tensor')), may hold values from -6 to 6
- adapter_index: int32 [2], replicated, may hold values from 0 to 7
- norm1_gain: bfloat16 [1280], replicated, may hold values from 0.099609375 to 1.8984375
- norm1_shift: bfloat16 [1280], replicated, may hold values from -2.5 to 2.5
- qkv_weight: bfloat16 [1280, 3, 1280], P(None, None, 'tensor'), may hold values from -0.15625 to 0.15625
- qkv_bias: bfloat16 [3, 1280], P(None, 'tensor'), may hold values from -2.5 to 2.5
- rel_pos_h: bfloat16 [27, 80], replicated, may hold values from -1.25 to 1.25
- rel_pos_w: bfloat16 [27, 80], replicated, may hold values from -1.25 to 1.25
- proj_weight: bfloat16 [1280, 1280], P('tensor'), may hold values from -0.625 to 0.625
- proj_bias: bfloat16 [1280], replicated, may hold values from -2.5 to 2.5
- norm2_gain: bfloat16 [1280], replicated, may hold values from 0.099609375 to 1.8984375
- norm2_shift: bfloat16 [1280], replicated, may hold values from -2.5 to 2.5
- lin1_weight: bfloat16 [1280, 5120], P(None, 'tensor'), may hold values from -0.15625 to 0.15625
- lin1_bias: bfloat16 [5120], P('tensor'), may hold values from -2.5 to 2.5
- lin2_weight: bfloat16 [5120, 1280], P('tensor'), may hold values from -0.078125 to 0.078125
- lin2_bias: bfloat16 [1280], replicated, may hold values from -2.5 to 2.5
- qkv_down: bfloat16 [8, 1280, 16], replicated, may hold values from -0.15625 to 0.15625
- qkv_up: bfloat16 [8, 16, 3, 1280], P(None, None, None, 'tensor'), may hold values from -1.5 to 1.5
- proj_down: bfloat16 [8, 1280, 16], P(None, 'tensor'), may hold values from -0.625 to 0.625
- proj_up: bfloat16 [8, 16, 1280], replicated, may hold values from -1.5 to 1.5
- lin1_down: bfloat16 [8, 1280, 16], replicated, may hold values from -0.15625 to 0.15625
- lin1_up: bfloat16 [8, 16, 5120], P(None, None, 'tensor'), may hold values from -1.5 to 1.5
- lin2_down: bfloat16 [8, 5120, 16], P(None, 'tensor'), may hold values from -0.078125 to 0.078125
- lin2_up: bfloat16 [8, 16, 1280], replicated, may hold values from -1.5 to 1.5
Outputs:
- output: bfloat16 [10976, 1280], P(('dp', 'tensor'))
- grad_tokens: bfloat16 [10976, 1280], P(('dp', 'tensor'))
- grad_qkv_down: float32 [8, 1280, 16], replicated
- grad_qkv_up: float32 [8, 16, 3, 1280], P(None, None, None, 'tensor')
- grad_proj_down: float32 [8, 1280, 16], P(None, 'tensor')
- grad_proj_up: float32 [8, 16, 1280], replicated
- grad_lin1_down: float32 [8, 1280, 16], replicated
- grad_lin1_up: float32 [8, 16, 5120], P(None, None, 'tensor')
- grad_lin2_down: float32 [8, 5120, 16], P(None, 'tensor')
- grad_lin2_up: float32 [8, 16, 1280], replicated
Inputs may be any that keep to these rules, and one draw needn't show every extreme that they name: `adapter_index`: one adapter for each image.
All inputs are finite; a program needn't handle non-finite values.
Results may differ from a plain program's by a relative error of at most 0.019.
Values may be sent and summed in bfloat16 or wider, within the bound.
A program may use at most 256 MiB of HBM per device.

v0:
```python
import jax
import jax.numpy as jnp
from jax import lax
from jax.sharding import PartitionSpec as P

HEAD_DIM = 80
WIN = 14
SIDE = 64
RANK = 16
ADAPTERS = 8
WIN_DEV = 7
GROUP = 4
GRID = 5
HIGH = lax.Precision.HIGHEST
ADAPT = 0.5
EPS = 1e-06


def fast_dot(first_op, second_op):
    return jnp.dot(first_op, second_op, preferred_element_type=jnp.float32)


def trans_dot(first_op, second_op):
    return lax.dot_general(
        first_op, second_op, (((1,), (1,)), ((), ())), preferred_element_type=jnp.float32
    )


def exact_dot(first_op, second_op):
    return jnp.dot(first_op, second_op.astype(jnp.float32), precision=HIGH)


def cross_dot(first_op, second_op):
    return lax.dot_general(
        first_op.astype(jnp.float32),
        second_op.astype(jnp.float32),
        (((0,), (0,)), ((), ())),
        precision=HIGH,
    )


def window_mask(first_slot, count_all):
    position = jnp.arange(count_all, dtype=jnp.int32)
    slot_index = first_slot + position // (WIN * WIN)
    within = position % (WIN * WIN)
    image_row = slot_index // GRID * WIN + within // WIN
    image_col = slot_index % GRID * WIN + within % WIN
    inside = (slot_index < GRID * GRID) & (image_row < SIDE) & (image_col < SIDE)
    return jnp.where(inside, 1.0, 0.0).astype(jnp.float32)[:, None]


def offset_table(position_table):
    offsets = (jnp.arange(WIN)[:, None] - jnp.arange(WIN)[None, :] + WIN - 1).reshape(-1)
    one_hot = (offsets[:, None] == jnp.arange(2 * WIN - 1)[None, :]).astype(jnp.float32)
    return exact_dot(one_hot, position_table).reshape(WIN, WIN, -1).astype(jnp.bfloat16)


def norm_parts(values):
    row_mean = jnp.mean(values, axis=-1, keepdims=True)
    centered = values - row_mean
    inv_std = lax.rsqrt(jnp.mean(centered * centered, axis=-1, keepdims=True) + EPS)
    return (centered * inv_std, inv_std)


def norm_back(grad_in, normalized, inv_std, norm_gain):
    scaled = grad_in * norm_gain
    return inv_std * (
        scaled
        - jnp.mean(scaled, axis=-1, keepdims=True)
        - normalized * jnp.mean(scaled * normalized, axis=-1, keepdims=True)
    )


def window_scores(queries, key_win, table_h, table_w):
    win_count, head_count = (queries.shape[0], queries.shape[1])
    tokens_win = WIN * WIN
    base_scores = jnp.einsum(
        "nhqc,nhkc->nhqk",
        queries.reshape(win_count, head_count, tokens_win, -1),
        key_win.reshape(win_count, head_count, tokens_win, -1),
        preferred_element_type=jnp.float32,
    ) * HEAD_DIM ** (-0.5)
    rel_rows = jnp.einsum("nhabc,akc->nhabk", queries, table_h, preferred_element_type=jnp.float32)
    rel_cols = jnp.einsum("nhabc,bkc->nhabk", queries, table_w, preferred_element_type=jnp.float32)
    scores = (
        base_scores.reshape(win_count, head_count, WIN, WIN, WIN, WIN)
        + rel_rows[:, :, :, :, :, None]
        + rel_cols[:, :, :, :, None, :]
    )
    return scores.reshape(win_count, head_count, tokens_win, tokens_win)


def attention_back(queries, key_win, value_win, log_total, grad_att, table_h, table_w):
    win_count, head_count = (queries.shape[0], queries.shape[1])
    tokens_win = WIN * WIN
    probs = jnp.exp(window_scores(queries, key_win, table_h, table_w) - log_total)
    grad_rows = grad_att.reshape(win_count, head_count, tokens_win, -1)
    dprob = jnp.einsum(
        "nhqc,nhkc->nhqk",
        grad_rows,
        value_win.reshape(win_count, head_count, tokens_win, -1),
        preferred_element_type=jnp.float32,
    )
    dvalues = jnp.einsum(
        "nhqk,nhqc->nhkc", probs.astype(jnp.bfloat16), grad_rows, preferred_element_type=jnp.float32
    )
    inner_sum = jnp.sum(probs * dprob, axis=-1, keepdims=True)
    dscore = (probs * (dprob - inner_sum)).astype(jnp.bfloat16)
    dqueries = jnp.einsum(
        "nhqk,nhkc->nhqc",
        dscore,
        key_win.reshape(win_count, head_count, tokens_win, -1),
        preferred_element_type=jnp.float32,
    ) * HEAD_DIM ** (-0.5)
    dkeys = jnp.einsum(
        "nhqk,nhqc->nhkc",
        dscore,
        queries.reshape(win_count, head_count, tokens_win, -1),
        preferred_element_type=jnp.float32,
    ) * HEAD_DIM ** (-0.5)
    dscore_six = dscore.astype(jnp.float32).reshape(win_count, head_count, WIN, WIN, WIN, WIN)
    from_rows = jnp.einsum(
        "nhabk,akc->nhabc", jnp.sum(dscore_six, axis=5), table_h.astype(jnp.float32), precision=HIGH
    )
    from_cols = jnp.einsum(
        "nhabk,bkc->nhabc", jnp.sum(dscore_six, axis=4), table_w.astype(jnp.float32), precision=HIGH
    )
    dqueries = dqueries.reshape(queries.shape) + from_rows + from_cols
    return (
        dqueries.astype(jnp.bfloat16),
        dkeys.reshape(queries.shape).astype(jnp.bfloat16),
        dvalues.reshape(queries.shape).astype(jnp.bfloat16),
    )


def on_device(
    tokens,
    grad_out,
    adapter_index,
    norm1_gain,
    norm1_shift,
    qkv_weight,
    qkv_bias,
    rel_pos_h,
    rel_pos_w,
    proj_weight,
    proj_bias,
    norm2_gain,
    norm2_shift,
    lin1_weight,
    lin1_bias,
    lin2_weight,
    lin2_bias,
    qkv_down,
    qkv_up,
    proj_down,
    proj_up,
    lin1_down,
    lin1_up,
    lin2_down,
    lin2_up,
):
    tensor_size = lax.axis_size("tensor")
    row_count = tokens.shape[0]
    full_rows = row_count * tensor_size
    dp_place = lax.axis_index("dp")
    tensor_place = lax.axis_index("tensor")
    valid_full = window_mask(dp_place % GROUP * WIN_DEV, full_rows)
    valid_local = lax.dynamic_slice_in_dim(valid_full, tensor_place * row_count, row_count, 0)
    image_place = dp_place // GROUP
    pick = jnp.sum(jnp.where(jnp.arange(adapter_index.shape[0]) == image_place, adapter_index, 0))
    slot_hot = jnp.where(jnp.arange(ADAPTERS) == pick, 1.0, 0.0).astype(jnp.float32)

    def select(table_all):
        return lax.dynamic_index_in_dim(table_all, pick, 0, keepdims=False)

    def into_slot(term):
        return slot_hot.reshape((-1,) + (1,) * term.ndim) * term[None]

    head_local = qkv_weight.shape[2] // HEAD_DIM
    width_local = qkv_weight.shape[2]

    def to_windows(values):
        return values.reshape(-1, WIN, WIN, head_local, HEAD_DIM).transpose(0, 3, 1, 2, 4)

    def from_windows(values):
        return values.transpose(0, 2, 3, 1, 4).reshape(full_rows, -1)

    gain_one = norm1_gain.astype(jnp.float32)
    gain_two = norm2_gain.astype(jnp.float32)
    table_h = offset_table(rel_pos_h)
    table_w = offset_table(rel_pos_w)
    a_qkv = select(qkv_down)
    b_qkv = select(qkv_up).reshape(RANK, -1)
    a_proj = select(proj_down)
    b_proj = select(proj_up)
    a_lin1 = select(lin1_down)
    b_lin2 = select(lin2_up)
    qkv_flat = qkv_weight.reshape(qkv_weight.shape[0], -1)
    x_local = tokens.astype(jnp.float32)
    normal_one, inv_one = norm_parts(x_local)
    xn1_local = (valid_local * (normal_one * gain_one + norm1_shift.astype(jnp.float32))).astype(
        jnp.bfloat16
    )
    xn1 = lax.all_gather(xn1_local, "tensor", axis=0, tiled=True)
    down_q = fast_dot(xn1, a_qkv)
    qkv = (
        fast_dot(xn1, qkv_flat)
        + qkv_bias.astype(jnp.float32).reshape(-1)
        + ADAPT * exact_dot(down_q, b_qkv)
    )
    qkv = qkv.astype(jnp.bfloat16).reshape(full_rows, 3, width_local)
    queries = to_windows(qkv[:, 0])
    key_win = to_windows(qkv[:, 1])
    value_win = to_windows(qkv[:, 2])
    win_count = queries.shape[0]
    tokens_win = WIN * WIN
    scores = window_scores(queries, key_win, table_h, table_w)
    row_max = jnp.max(scores, axis=-1, keepdims=True)
    exponent = jnp.exp(scores - row_max)
    row_total = jnp.sum(exponent, axis=-1, keepdims=True)
    log_total = row_max + jnp.log(row_total)
    probs = exponent / row_total
    attended = jnp.einsum(
        "nhqk,nhkc->nhqc",
        probs.astype(jnp.bfloat16),
        value_win.reshape(win_count, head_local, tokens_win, -1),
        preferred_element_type=jnp.float32,
    )
    att = from_windows(attended.reshape(queries.shape)).astype(jnp.bfloat16)
    down_p = fast_dot(att, a_proj)
    down_part = down_p
    branch_a = lax.psum_scatter(
        (fast_dot(att, proj_weight) + ADAPT * exact_dot(down_part, b_proj)).astype(jnp.bfloat16),
        "tensor",
        scatter_dimension=0,
        tiled=True,
    ).astype(jnp.float32)
    middle = x_local + valid_local * (branch_a + proj_bias.astype(jnp.float32))
    normal_two, inv_two = norm_parts(middle)
    xn2_local = (normal_two * gain_two + norm2_shift.astype(jnp.float32)).astype(jnp.bfloat16)
    xn2 = lax.all_gather(xn2_local, "tensor", axis=0, tiled=True)
    w_lin1, c_lin1, b_lin1, a_lin2, w_lin2 = (
        lin1_weight,
        lin1_bias,
        select(lin1_up),
        select(lin2_down),
        lin2_weight,
    )
    down_1 = fast_dot(xn2, a_lin1)
    hidden_pre = (
        fast_dot(xn2, w_lin1) + c_lin1.astype(jnp.float32) + ADAPT * exact_dot(down_1, b_lin1)
    )
    gelu_value, gelu_grad = jax.vjp(
        lambda values: jax.nn.gelu(values, approximate=False), hidden_pre
    )
    hidden_act = gelu_value.astype(jnp.bfloat16)
    down_2 = fast_dot(hidden_act, a_lin2)
    down_part = down_2
    branch_m = lax.psum_scatter(
        (fast_dot(hidden_act, w_lin2) + ADAPT * exact_dot(down_part, b_lin2)).astype(jnp.bfloat16),
        "tensor",
        scatter_dimension=0,
        tiled=True,
    ).astype(jnp.float32)
    output = (middle + valid_local * (branch_m + lin2_bias.astype(jnp.float32))).astype(
        jnp.bfloat16
    )
    dout_f = grad_out.astype(jnp.float32)
    dy2_local = (valid_local * dout_f).astype(jnp.bfloat16)
    dy2 = lax.all_gather(dy2_local, "tensor", axis=0, tiled=True)
    up2 = trans_dot(dy2, b_lin2)
    dact = trans_dot(dy2, w_lin2) + ADAPT * exact_dot(up2, a_lin2.T)
    dpre = gelu_grad(dact)[0].astype(jnp.bfloat16)
    up1 = trans_dot(dpre, b_lin1)
    grad_lin2_up_t = ADAPT * cross_dot(down_2, dy2)
    grad_lin2_down_t = ADAPT * cross_dot(hidden_act, up2)
    grad_lin1_up_t = ADAPT * cross_dot(down_1, dpre)
    grad_lin1_down_t = ADAPT * cross_dot(xn2, up1)
    up_part = up1
    dxn2 = lax.psum_scatter(
        (trans_dot(dpre, w_lin1) + ADAPT * exact_dot(up_part, a_lin1.T)).astype(jnp.bfloat16),
        "tensor",
        scatter_dimension=0,
        tiled=True,
    ).astype(jnp.float32)
    dmiddle = dout_f + norm_back(dxn2, normal_two, inv_two, gain_two)
    dya_local = (valid_local * dmiddle).astype(jnp.bfloat16)
    dya = lax.all_gather(dya_local, "tensor", axis=0, tiled=True)
    upp = trans_dot(dya, b_proj)
    datt = (trans_dot(dya, proj_weight) + ADAPT * exact_dot(upp, a_proj.T)).astype(jnp.bfloat16)
    grad_proj_up_t = ADAPT * cross_dot(down_p, dya)
    grad_proj_down_t = ADAPT * cross_dot(att, upp)
    dqueries, dkeys, dvalues = attention_back(
        queries, key_win, value_win, log_total, to_windows(datt), table_h, table_w
    )
    dqkv = jnp.stack(
        [from_windows(dqueries), from_windows(dkeys), from_windows(dvalues)], axis=1
    ).reshape(full_rows, -1)
    upq = trans_dot(dqkv, b_qkv)
    grad_qkv_up_t = (ADAPT * cross_dot(down_q, dqkv)).reshape(RANK, 3, -1)
    grad_qkv_down_t = ADAPT * cross_dot(xn1, upq)
    up_part = upq
    dxn1 = lax.psum_scatter(
        (trans_dot(dqkv, qkv_flat) + ADAPT * exact_dot(up_part, a_qkv.T)).astype(jnp.bfloat16),
        "tensor",
        scatter_dimension=0,
        tiled=True,
    ).astype(jnp.float32)
    grad_tokens = (dmiddle + norm_back(valid_local * dxn1, normal_one, inv_one, gain_one)).astype(
        jnp.bfloat16
    )
    grad_qkv_up, grad_proj_down, grad_lin1_up, grad_lin2_down = lax.psum(
        (
            into_slot(grad_qkv_up_t),
            into_slot(grad_proj_down_t),
            into_slot(grad_lin1_up_t),
            into_slot(grad_lin2_down_t),
        ),
        "dp",
    )
    grad_qkv_down, grad_proj_up, grad_lin1_down, grad_lin2_up = lax.psum(
        (
            into_slot(grad_qkv_down_t),
            into_slot(grad_proj_up_t),
            into_slot(grad_lin1_down_t),
            into_slot(grad_lin2_up_t),
        ),
        ("dp", "tensor"),
    )
    return (
        output,
        grad_tokens,
        grad_qkv_down,
        grad_qkv_up,
        grad_proj_down,
        grad_proj_up,
        grad_lin1_down,
        grad_lin1_up,
        grad_lin2_down,
        grad_lin2_up,
    )


def solution(mesh):
    placed = (
        P(("dp", "tensor"), None),
        P(("dp", "tensor"), None),
        P(),
        P(),
        P(),
        P(None, None, "tensor"),
        P(None, "tensor"),
        P(),
        P(),
        P("tensor", None),
        P(),
        P(),
        P(),
        P(None, "tensor"),
        P("tensor"),
        P("tensor", None),
        P(),
        P(),
        P(None, None, None, "tensor"),
        P(None, "tensor", None),
        P(),
        P(),
        P(None, None, "tensor"),
        P(None, "tensor", None),
        P(),
    )
    return jax.shard_map(
        on_device,
        mesh=mesh,
        in_specs=placed,
        out_specs=(
            P(("dp", "tensor"), None),
            P(("dp", "tensor"), None),
            P(),
            P(None, None, None, "tensor"),
            P(None, "tensor", None),
            P(),
            P(),
            P(None, None, "tensor"),
            P(None, "tensor", None),
            P(),
        ),
        check_vma=False,
    )
```

profile of v0, /device:TPU:0, one launch (start us, length us, event | category | flops | bytes accessed | tf_op | source)
XLA Modules:
  0.0 929.5 jit_solution(8334608292282891529)
XLA Ops:
  19.2 28.9 %all-gather.9.cloned.1.call-done = bf16[4,343,1280]{2,1,0:T(8,128)(2,1)} async-done(((bf16[1,343,1280]{2,1,0:T(8,128)(2,1)}), bf16[4,343,1280]{2,1,0:T(8,128)(2,1)}) %all-gather.9.cloned.1.call-update) | async-done | bytes 3512336 | tf_op jit(solution)/shard_map/all_gather | solution.py:205
  48.1 4.7 reshape.204
  56.0 5.7 fusion.149
  100.1 6.8 convolution_bitcast_fusion.2
  106.9 5.8 copy.101
  112.7 6.8 convolution_bitcast_fusion.1
  119.5 6.3 copy.105
  125.8 16.1 %add.258 = f32[7,4,14,14,14,14]{5,4,3,2,1,0:T(8,128)} broadcast(f32[7,4,14,14,14]{4,3,2,1,0:T(8,128)} %copy.105), dimensions={0,1,2,3,5} | broadcast | bytes 4609920 | tf_op jit(solution)/shard_map/add | solution.py:86
  141.9 26.9 %add.259 = f32[7,4,196,196]{3,2,1,0:T(8,128)} reshape(f32[7,4,14,14,14,14]{5,4,3,2,1,0:T(8,128)} %add.258) | data formatting | bytes 8605184 | tf_op jit(solution)/shard_map/add | solution.py:86
  168.8 6.8 copy.106
  175.6 16.6 %add.255 = f32[7,4,14,14,14,14]{5,4,3,2,1,0:T(8,128)} broadcast(f32[7,4,14,14,14]{4,3,2,1,0:T(8,128)} %copy.101), dimensions={0,1,2,3,4} | broadcast | bytes 4609920 | tf_op jit(solution)/shard_map/add | solution.py:86
  192.2 26.9 %add.256 = f32[7,4,196,196]{3,2,1,0:T(8,128)} reshape(f32[7,4,14,14,14,14]{5,4,3,2,1,0:T(8,128)} %add.255) | data formatting | bytes 8605184 | tf_op jit(solution)/shard_map/add | solution.py:86
  219.1 6.5 copy.102
  225.5 6.3 fusion.148
  248.9 5.7 fusion.13
  254.6 35.5 %fusion = bf16[344,1280]{1,0:T(8,128)(2,1)} fusion(bf16[1372,1280]{1,0:T(8,128)(2,1)} %fusion.13), kind=kCustom, calls=%all-reduce-scatter | all-reduce-scatter fusion | flops 1761281 | bytes 4393472
  293.5 6.1 concatenate
  306.8 33.4 %all-gather.13.cloned.1.call-done = bf16[4,343,1280]{2,1,0:T(8,128)(2,1)} async-done(((bf16[1,343,1280]{2,1,0:T(8,128)(2,1)}), bf16[4,343,1280]{2,1,0:T(8,128)(2,1)}) %all-gather.13.cloned.1.call-update) | async-done | bytes 3512336 | tf_op jit(solution)/shard_map/all_gather | solution.py:271
  340.2 4.7 reshape.208
  348.1 9.0 fusion.152
  357.2 15.9 %all-gather.11.cloned.1.call-done = bf16[4,343,1280]{2,1,0:T(8,128)(2,1)} async-done(((bf16[1,343,1280]{2,1,0:T(8,128)(2,1)}), bf16[4,343,1280]{2,1,0:T(8,128)(2,1)}) %all-gather.11.cloned.1.call-update) | async-done | bytes 3512336 | tf_op jit(solution)/shard_map/all_gather | solution.py:242
  373.1 4.8 reshape.206
  381.1 4.9 convolution_add_fusion
  386.0 22.5 %multiply_convert_fusion = (bf16[1372,1280]{1,0:T(8,128)(2,1)}, f32[1372,1280]{1,0:T(8,128)S(1)}, f32[1372,1280]{1,0:T(8,128)}) fusion(f32[1372,1280]{1,0:T(8,128)S(1)} %convolution_add_fusion, f32[1372,16]{0,1:T(8,128)S(1)} %fusion.81, bf16[8,16,1280]{2,1,0:T(8,128)(2,1)} %param.47, s32[]{:T(128)S(6)} %select_n.86), kind=kOutput, calls=%fused_computation.21 | convolution fusion | flops 454845440 | bytes 24715012 | tf_op jit(solution)/shard_map/dot_general | solution.py:30
  408.5 9.7 %add_convert_fusion = bf16[1372,1280]{1,0:T(8,128)(2,1)S(1)} fusion(f32[1372,1280]{1,0:T(8,128)S(1)} %get-tuple-element.31, f32[1372,1280]{1,0:T(8,128)S(1)} %bitcast.198, f32[1372,16]{0,1:T(8,128)S(1)} %fusion.71, f32[1372,1280]{1,0:T(8,128)} %get-tuple-element.47, bf16[8,1280,16]{1,2,0:T(8,128)(2,1)} %param.48, s32[]{:T(128)S(6)} %select_n.86), kind=kOutput, calls=%fused_computation.20 | convolution fusion | flops 365281280 | bytes 24735492 | tf_op jit(solution)/shard_map/dot_general | solution.py:30
  420.0 4.8 fusion.153
  424.8 6.0 fusion.11
  430.9 35.2 %fusion.2 = bf16[344,1280]{1,0:T(8,128)(2,1)} fusion(bf16[1372,1280]{1,0:T(8,128)(2,1)} %fusion.11), kind=kCustom, calls=%all-reduce-scatter.2 | all-reduce-scatter fusion | flops 1761281 | bytes 4393472
  469.0 6.7 concatenate.2
  497.3 4.8 fusion.151
  502.1 6.5 fusion.12
  508.5 9.3 all-gather.15.cloned.1.call-done
  517.8 4.7 reshape.210
  544.0 5.2 fusion.55
  549.1 4.3 multiply_reduce_fusion
  559.1 5.2 copy.117
  583.8 4.5 copy.116
  588.3 26.1 %reshape.202 = f32[7,4,14,14,14,14]{5,4,3,2,1,0:T(8,128)} reshape(f32[7,4,196,196]{3,2,1,0:T(8,128)} %copy.117) | data formatting | bytes 8605184 | tf_op jit(solution)/shard_map/reshape | solution.py:121
  614.4 19.9 %fusion.144 = (f32[7,4,14,14,14]{4,3,2,1,0:T(8,128)}, f32[7,4,14,14,14]{4,3,2,1,0:T(8,128)}) fusion(f32[7,4,14,14,14,14]{5,4,3,2,1,0:T(8,128)} %reshape.202), kind=kLoop, calls=%fused_computation.232 | loop fusion | flops 1997632 | bytes 4917248 | tf_op jit(solution)/shard_map/reduce_sum | solution.py:123
  634.3 4.4 fusion.23
  666.6 6.4 convolution_bitcast_fusion
  673.0 5.7 fusion.10
  678.7 68.8 %fusion.145 = (bf16[344,1280]{1,0:T(8,128)(2,1)}, bf16[344,1280]{1,0:T(8,128)(2,1)}) fusion(bf16[1372,1280]{1,0:T(8,128)(2,1)} %fusion.12, bf16[1372,1280]{1,0:T(8,128)(2,1)} %fusion.10), kind=kCustom, calls=%all-reduce-scatter.4 | all-reduce-scatter fusion | flops 3522561 | bytes 8786432
  753.5 6.1 concatenate.3
  759.6 6.1 concatenate.1
  768.0 5.6 fusion.45
  773.5 31.3 %all-reduce.14.cloned.1.call-done = (f32[8,1280,16]{1,2,0:T(8,128)}, f32[8,16,1280]{2,1,0:T(8,128)}, f32[8,1280,16]{1,2,0:T(8,128)}, f32[8,16,1280]{2,1,0:T(8,128)}) async-done(((f32[8,1280,16]{1,2,0:T(8,128)}, f32[8,16,1280]{2,1,0:T(8,128)}, f32[8,1280,16]{1,2,0:T(8,128)}, f32[8,16,1280]{2,1,0:T(8,128)}), (f32[8,1280,16]{1,2,0:T(8,128)}, f32[8,16,1280]{2,1,0:T(8,128)}, f32[8,1280,16]{1,2,0:T(8,128)}, ...) | async-done | bytes 2621456 | tf_op jit(solution)/shard_map/psum | solution.py:322
  804.8 107.7 %all-reduce.16.cloned.1.call-done = (f32[8,16,3,320]{3,1,2,0:T(8,128)}, f32[8,320,16]{1,2,0:T(8,128)}, f32[8,16,1280]{2,1,0:T(8,128)}, f32[8,1280,16]{1,2,0:T(8,128)}) async-done(((f32[8,16,3,320]{3,1,2,0:T(8,128)}, f32[8,320,16]{1,2,0:T(8,128)}, f32[8,16,1280]{2,1,0:T(8,128)}, f32[8,1280,16]{1,2,0:T(8,128)}), (f32[8,16,3,320]{3,1,2,0:T(8,128)}, f32[8,320,16]{1,2,0:T(8,128)}, f32[8,16,1280]{2,1,0:T(8,128)}, ...) | async-done | bytes 1966096 | tf_op jit(solution)/shard_map/psum | solution.py:313
  (276 shorter events, 203.3 us)
Async XLA Ops:
  7.2 373.8 %copy-start = (bf16[1280,1280]{1,0:T(8,128)(2,1)S(1)}, bf16[1280,1280]{1,0:T(8,128)(2,1)}, u32[]{:S(2)}) copy-start(bf16[1280,1280]{1,0:T(8,128)(2,1)} %param.38) | copy-start | bytes 9830404
  7.2 7.4 copy-start.63
  7.2 9.3 %copy-start.58 = (bf16[3,320]{1,0:T(4,128)(2,1)S(1)}, bf16[3,320]{1,0:T(4,128)(2,1)}, u32[]{:S(2)}) copy-start(bf16[3,320]{1,0:T(4,128)(2,1)} %param.31) | copy-start | bytes 5764
  7.2 11.1 %copy-start.61 = (bf16[27,80]{1,0:T(8,128)(2,1)S(1)}, bf16[27,80]{1,0:T(8,128)(2,1)}, u32[]{:S(2)}) copy-start(bf16[27,80]{1,0:T(8,128)(2,1)} %param.33) | copy-start | bytes 12964
  7.2 11.5 %copy-start.62 = (bf16[27,80]{1,0:T(8,128)(2,1)S(1)}, bf16[27,80]{1,0:T(8,128)(2,1)}, u32[]{:S(2)}) copy-start(bf16[27,80]{1,0:T(8,128)(2,1)} %param.32) | copy-start | bytes 12964
  7.2 40.8 %all-gather.9.cloned.1.call-start = ((), (), s32[]{:S(2)}) async-start(), calls=%async_computation | async-start | bytes 4403200 | tf_op jit(solution)/shard_map/all_gather | solution.py:205
  8.8 8.6 copy-start.49
  10.4 7.0 copy-start.51
  11.1 6.3 copy-start.47
  14.5 325.7 %all-gather.13.cloned.1.call-start = ((), (), s32[]{:S(2)}) async-start(), calls=%async_computation.2 | async-start | bytes 4403200 | tf_op jit(solution)/shard_map/all_gather | solution.py:271
  18.3 43.4 %copy-start.45 = (bf16[16,960]{1,0:T(8,128)(2,1)}, bf16[16,960]{1,0:T(8,128)(2,1)S(1)}, u32[]{:S(2)}) copy-start(bf16[16,960]{1,0:T(8,128)(2,1)S(1)} %reshape.189) | copy-start | bytes 92164
  18.7 93.9 %copy-start.40 = (bf16[14,14,80,1,1]{2,1,0,3,4:T(8,128)(2,1)}, bf16[14,14,80,1,1]{2,1,0,3,4:T(8,128)(2,1)S(1)}, u32[]{:S(2)}) copy-start(bf16[14,14,80,1,1]{2,1,0,3,4:T(8,128)(2,1)S(1)} %reshape.212) | copy-start | bytes 94084
  19.2 80.9 %copy-start.42 = (bf16[14,14,80,1,1]{2,1,0,3,4:T(8,128)(2,1)}, bf16[14,14,80,1,1]{2,1,0,3,4:T(8,128)(2,1)S(1)}, u32[]{:S(2)}) copy-start(bf16[14,14,80,1,1]{2,1,0,3,4:T(8,128)(2,1)S(1)} %reshape.211) | copy-start | bytes 94084
  55.9 5.8 copy-start.27
  254.6 37.5 %copy-start.53 = (bf16[1280]{0:T(1024)(128)(2,1)S(1)}, bf16[1280]{0:T(1024)(128)(2,1)}, u32[]{:S(2)}) copy-start(bf16[1280]{0:T(1024)(128)(2,1)} %param.35) | copy-start | bytes 7684
  254.6 37.6 %copy-start.54 = (bf16[1280]{0:T(1024)(128)(2,1)S(1)}, bf16[1280]{0:T(1024)(128)(2,1)}, u32[]{:S(2)}) copy-start(bf16[1280]{0:T(1024)(128)(2,1)} %param.36) | copy-start | bytes 7684
  254.6 37.6 %copy-start.55 = (bf16[1280]{0:T(1024)(128)(2,1)S(1)}, bf16[1280]{0:T(1024)(128)(2,1)}, u32[]{:S(2)}) copy-start(bf16[1280]{0:T(1024)(128)(2,1)} %param.37) | copy-start | bytes 7684
  254.6 37.6 %copy-start.59 = (u32[32]{0:T(128)S(1)}, u32[32]{0:T(128)}, u32[]{:S(2)}) copy-start(u32[32]{0:T(128)} %constant.209) | copy-start | bytes 388
  290.8 2.6 collective-permute-start
  306.0 67.1 %all-gather.11.cloned.1.call-start = ((), (), s32[]{:S(2)}) async-start(), calls=%async_computation.1 | async-start | bytes 4403200 | tf_op jit(solution)/shard_map/all_gather | solution.py:242
  306.7 211.1 %all-gather.15.cloned.1.call-start = ((), (), s32[]{:S(2)}) async-start(), calls=%async_computation.3 | async-start | bytes 4403200 | tf_op jit(solution)/shard_map/all_gather | solution.py:289
  348.1 60.4 %copy-start.37 = (f32[1372,16]{0,1:T(8,128)}, f32[1372,16]{0,1:T(8,128)S(1)}, u32[]{:S(2)}) copy-start(f32[1372,16]{0,1:T(8,128)S(1)} %fusion.71) | copy-start | bytes 263428
  381.1 4.9 copy-start.38
  381.1 27.4 %slice-start.2 = ((s8[7045120]{0:T(1024)(128)(4,1)}), s8[4194304]{0:T(1024)(128)(4,1)S(1)}, s32[]{:S(2)}) async-start(s8[7045120]{0:T(1024)(128)(4,1)} %bitcast.197), calls=%async_computation.8 | async-start | bytes 8388608
  386.0 22.5 %slice-start.3 = ((s8[7045120]{0:T(1024)(128)(4,1)}), s8[2850816]{0:T(1024)(128)(4,1)S(1)}, s32[]{:S(2)}) async-start(s8[7045120]{0:T(1024)(128)(4,1)} %bitcast.197), calls=%async_computation.9 | async-start | bytes 5701632
  418.2 6.7 copy-start.15
  466.8 2.2 collective-permute-start.2
  483.1 321.8 %all-reduce.14.cloned.1.call-start = ((), (), s32[]{:S(2)}) async-start(), calls=%async_computation.4 | async-start | bytes 5242880 | tf_op jit(solution)/shard_map/psum | solution.py:322
  533.9 10.1 %copy-start.44 = (f32[7,4,196]{2,1,0:T(4,128)S(1)}, f32[7,4,196]{2,1,0:T(4,128)}, u32[]{:S(2)}) copy-start(f32[7,4,196]{2,1,0:T(4,128)} %log_add_fusion) | copy-start | bytes 65860
  544.0 5.2 copy-start.22
  544.0 5.2 copy-start.25
  544.0 9.5 %slice-start = ((s8[5734400]{0:T(1024)(128)(4,1)}), s8[4194304]{0:T(1024)(128)(4,1)S(1)}, s32[]{:S(2)}) async-start(s8[5734400]{0:T(1024)(128)(4,1)} %bitcast.182), calls=%async_computation.6 | async-start | bytes 8388608
  614.4 19.9 %copy-start.41 = (bf16[14,14,80,1,1]{2,1,0,3,4:T(8,128)(2,1)S(1)}, bf16[14,14,80,1,1]{2,1,0,3,4:T(8,128)(2,1)}, u32[]{:S(2)}) copy-start(bf16[14,14,80,1,1]{2,1,0,3,4:T(8,128)(2,1)} %copy-done.40) | copy-start | bytes 94084
  650.0 5.0 copy-start.46
  657.6 7.3 copy-start.35
  659.2 5.7 copy-start.36
  666.3 246.2 %all-reduce.16.cloned.1.call-start = ((), (), s32[]{:S(2)}) async-start(), calls=%async_computation.5 | async-start | bytes 4194304 | tf_op jit(solution)/shard_map/psum | solution.py:313
  678.7 74.8 %copy-start.57 = (bf16[1280]{0:T(1024)(128)(2,1)S(1)}, bf16[1280]{0:T(1024)(128)(2,1)}, u32[]{:S(2)}) copy-start(bf16[1280]{0:T(1024)(128)(2,1)} %param.41) | copy-start | bytes 7684
  747.5 18.1 %copy-start.48 = (f32[1280]{0:T(1024)S(1)}, f32[1280]{0:T(1024)}, u32[]{:S(2)}) copy-start(f32[1280]{0:T(1024)} %copy-done.47) | copy-start | bytes 15364
  747.5 18.1 %copy-start.50 = (f32[343]{0:T(512)S(1)}, f32[343]{0:T(512)}, u32[]{:S(2)}) copy-start(f32[343]{0:T(512)} %copy-done.49) | copy-start | bytes 4120
  747.5 18.1 %copy-start.52 = (f32[343]{0:T(512)S(1)}, f32[343]{0:T(512)}, u32[]{:S(2)}) copy-start(f32[343]{0:T(512)} %copy-done.51) | copy-start | bytes 4120
  748.3 5.2 collective-permute-start.3
  750.3 9.2 collective-permute-start.1
  912.5 5.7 copy-start.32
  912.5 6.6 copy-start.31
  912.5 7.4 copy-start.34
  912.5 8.2 copy-start.33
  914.7 7.0 copy-start.30
  (30 other events, 95.6 us)
Sparse Core Ops, SparseCore 0:
  14.7 33.3 all-gather.8
  306.1 34.0 all-gather.12
  342.4 30.6 all-gather.10
  483.2 34.5 all-gather.14
  666.4 138.3 all-reduce.13
  810.3 102.1 all-reduce.15
where the time goes:
time: 941 us; the launch traced here: 930 us
  local copies, waits for them, and re-layouts  291 us (31%)
  waiting for transfers between devices  228 us (24%)
  matrix products  184 us (20%)
  blocking collectives  140 us (15%)
  other arithmetic  61.4 us (7%)
  between operations  17.9 us (2%)
    unnamed x3, blocking collectives  140 us
    psum x1, waiting for transfers between devices, on_device(): lax.psum((into_slot(grad_qkv_up_t), into_slot(grad_proj_down_t), into_slo...  108 us
    add x6, local copies, waits for them, and re-layouts, window_scores(): base_scores.reshape(win_count, head_count, WIN, WIN, WIN, WIN)  99.8 us
    unnamed x160, local copies, waits for them, and re-layouts  66.6 us
    dot_general x10, matrix products, exact_dot(): return jnp.dot(first_op, second_op.astype(jnp.float32), precision=HIGH)  62.1 us
    all_gather x1, waiting for transfers between devices, on_device(): dy2 = lax.all_gather(dy2_local, 'tensor', axis=0, tiled=True)  33.4 us
    reshape x2, local copies, waits for them, and re-layouts, attention_back(): dscore.astype(jnp.float32)  31.3 us
    psum x1, waiting for transfers between devices, on_device(): lax.psum((into_slot(grad_qkv_down_t), into_slot(grad_proj_up_t), into_slo...  31.3 us
  transfers between devices with their start and end apart: 10, of which 7 were waited for; matrix products, arithmetic and copies ran while one was open for 16% of the time, Pallas kernels for 0%

commit v1 on v0

--- a/solution.py
+++ b/solution.py
@@ -2,6 +2,7 @@
 import jax.numpy as jnp
 from jax import lax
 from jax.sharding import PartitionSpec as P
+from jax.lax import axis_index, axis_size, ppermute
 
 HEAD_DIM = 80
 WIN = 14
@@ -14,6 +15,24 @@
 HIGH = lax.Precision.HIGHEST
 ADAPT = 0.5
 EPS = 1e-06
+
+
+def _read_inputs(t0, axis_tag="tensor"):
+    slots = axis_size(axis_tag)
+    trail = []
+    for it in range(slots):
+        trail.append((it, (it + 1) % slots))
+    shelf = []
+    for it in range(slots):
+        shelf.append((it, (it - 1) % slots))
+    local_next, u1 = ([t0], [t0])
+    for _ in range(slots // 2):
+        local_next.append(ppermute(local_next[-1], axis_tag, trail))
+    for _ in range((slots - 1) // 2):
+        u1.append(ppermute(u1[-1], axis_tag, shelf))
+    reached = jnp.concatenate([*local_next[::-1], *u1[1:]], axis=0)
+    front = jnp.roll(reached, (axis_index(axis_tag) - slots // 2) * t0.shape[0], axis=0)
+    return front
 
 
 def fast_dot(first_op, second_op):
@@ -268,7 +287,7 @@
     )
     dout_f = grad_out.astype(jnp.float32)
     dy2_local = (valid_local * dout_f).astype(jnp.bfloat16)
-    dy2 = lax.all_gather(dy2_local, "tensor", axis=0, tiled=True)
+    dy2 = _read_inputs(dy2_local)
     up2 = trans_dot(dy2, b_lin2)
     dact = trans_dot(dy2, w_lin2) + ADAPT * exact_dot(up2, a_lin2.T)
     dpre = gelu_grad(dact)[0].astype(jnp.bfloat16)

time: 941 us -> 983 us (1.045)
  local copies, waits for them, and re-layouts: 291 us -> 330 us
  waiting for transfers between devices: 228 us -> 210 us
  starting transfers between devices: 8.19 us -> 23.5 us
    concatenate x0 -> x1, local copies, waits for them, and re-layouts: none -> 42.9 us  [_read_inputs(): jnp.roll(reached, (axis_index(axis_tag) - slots // 2) * t0.shape[0], axis=0)]
    ppermute x0 -> x3, waiting for transfers between devices: none -> 35.2 us  [the longest x2 35.2 us: _read_inputs(): local_next.append(ppermute(local_next[-1], axis_tag, trail))]
    all_gather x1 -> x0, waiting for transfers between devices: 33.4 us -> none  [on_device(): dy2 = lax.all_gather(dy2_local, 'tensor', axis=0, tiled=True)]
    all_gather x1, waiting for transfers between devices: 15.9 us -> 0.01 us  [on_device(): xn2 = lax.all_gather(xn2_local, 'tensor', axis=0, tiled=True)]
    ppermute x0 -> x3, starting transfers between devices: none -> 15.4 us  [the longest x2 15.3 us: _read_inputs(): local_next.append(ppermute(local_next[-1], axis_tag, trail))]
    unnamed x160 -> x169, local copies, waits for them, and re-layouts: 66.6 us -> 62.7 us
  transfers between devices with their start and end apart: 10 -> 12, of which waited for: 7 -> 7; matrix products, arithmetic and copies ran while one was open for 16% -> 19% of each run, Pallas kernels for 0% -> 0%
where the time goes in v1:
time: 983 us; the launch traced here: 970 us
  local copies, waits for them, and re-layouts  330 us (34%)
  waiting for transfers between devices  210 us (21%)
  matrix products  186 us (19%)
  blocking collectives  141 us (14%)
  other arithmetic  62.6 us (6%)
  starting transfers between devices  23.5 us (2%)
  between operations  17.5 us (2%)
    unnamed x3, blocking collectives  141 us
    psum x1, waiting for transfers between devices, on_device(): lax.psum((into_slot(grad_qkv_up_t), into_slot(grad_proj_down_t), into_slo...  108 us
    add x6, local copies, waits for them, and re-layouts, window_scores(): base_scores.reshape(win_count, head_count, WIN, WIN, WIN, WIN)  99.7 us
    unnamed x169, local copies, waits for them, and re-layouts  62.7 us
    dot_general x10, matrix products, exact_dot(): return jnp.dot(first_op, second_op.astype(jnp.float32), precision=HIGH)  58.1 us
    concatenate x1, local copies, waits for them, and re-layouts, _read_inputs(): jnp.roll(reached, (axis_index(axis_tag) - slots // 2) * t0.shape[0], axis=0)  42.9 us
    ppermute x2, waiting for transfers between devices, _read_inputs(): local_next.append(ppermute(local_next[-1], axis_tag, trail))  35.2 us
    dot_general x8, matrix products, trans_dot(): lax.dot_general(first_op, second_op, (((1,), (1,)), ((), ())), preferred_...  34 us
  transfers between devices with their start and end apart: 12, of which 7 were waited for; matrix products, arithmetic and copies ran while one was open for 19% of the time, Pallas kernels for 0%

profile of v1, /device:TPU:0, one launch (start us, length us, event | category | flops | bytes accessed | tf_op | source)
XLA Modules:
  0.0 970.3 jit_solution(6587987041403573618)
XLA Ops:
  19.1 29.0 %all-gather.7.cloned.1.call-done = bf16[4,343,1280]{2,1,0:T(8,128)(2,1)} async-done(((bf16[1,343,1280]{2,1,0:T(8,128)(2,1)}), bf16[4,343,1280]{2,1,0:T(8,128)(2,1)}) %all-gather.7.cloned.1.call-update) | async-done | bytes 3512336 | tf_op jit(solution)/shard_map/all_gather | solution.py:224
  48.1 4.7 reshape.204
  56.0 5.7 fusion.156
  100.0 6.8 convolution_bitcast_fusion.2
  106.8 5.7 copy.101
  112.6 6.8 convolution_bitcast_fusion.1
  119.4 6.3 copy.105
  125.7 16.1 %add.269 = f32[7,4,14,14,14,14]{5,4,3,2,1,0:T(8,128)} broadcast(f32[7,4,14,14,14]{4,3,2,1,0:T(8,128)} %copy.105), dimensions={0,1,2,3,5} | broadcast | bytes 4609920 | tf_op jit(solution)/shard_map/add | solution.py:105
  141.8 26.9 %add.270 = f32[7,4,196,196]{3,2,1,0:T(8,128)} reshape(f32[7,4,14,14,14,14]{5,4,3,2,1,0:T(8,128)} %add.269) | data formatting | bytes 8605184 | tf_op jit(solution)/shard_map/add | solution.py:105
  168.7 6.9 copy.106
  175.6 16.6 %add.266 = f32[7,4,14,14,14,14]{5,4,3,2,1,0:T(8,128)} broadcast(f32[7,4,14,14,14]{4,3,2,1,0:T(8,128)} %copy.101), dimensions={0,1,2,3,4} | broadcast | bytes 4609920 | tf_op jit(solution)/shard_map/add | solution.py:105
  192.1 26.9 %add.267 = f32[7,4,196,196]{3,2,1,0:T(8,128)} reshape(f32[7,4,14,14,14,14]{5,4,3,2,1,0:T(8,128)} %add.266) | data formatting | bytes 8605184 | tf_op jit(solution)/shard_map/add | solution.py:105
  219.0 6.4 copy.102
  225.4 6.3 fusion.155
  249.5 5.8 fusion.12
  255.3 35.5 %fusion = bf16[344,1280]{1,0:T(8,128)(2,1)} fusion(bf16[1372,1280]{1,0:T(8,128)(2,1)} %fusion.12), kind=kCustom, calls=%all-reduce-scatter | all-reduce-scatter fusion | flops 1761281 | bytes 4393472
  294.1 6.0 concatenate.7
  309.1 19.4 %collective-permute-done = bf16[343,1280]{1,0:T(8,128)(2,1)} collective-permute-done((bf16[343,1280]{1,0:T(8,128)(2,1)}, bf16[343,1280]{1,0:T(8,128)(2,1)}, u32[]{:S(2)}, u32[]{:S(2)}) %collective-permute-start) | collective-permute-done | bytes 878112 | tf_op jit(solution)/shard_map/ppermute | solution.py:30
  328.5 12.9 %collective-permute-start.1 = (bf16[343,1280]{1,0:T(8,128)(2,1)}, bf16[343,1280]{1,0:T(8,128)(2,1)}, u32[]{:S(2)}, u32[]{:S(2)}) collective-permute-start(bf16[343,1280]{1,0:T(8,128)(2,1)} %collective-permute-done), channel_id=1, source_target_pairs={{0,1},{1,2},{2,3},{3,0},{4,5},{5,6},{6,7},{7,4},{8,9},{9,10},{10,1... | collective-permute-start | bytes 2634248 | tf_op jit(solution)/shard_map/ppermute | solution.py:30
  341.5 15.8 %collective-permute-done.1 = bf16[343,1280]{1,0:T(8,128)(2,1)} collective-permute-done((bf16[343,1280]{1,0:T(8,128)(2,1)}, bf16[343,1280]{1,0:T(8,128)(2,1)}, u32[]{:S(2)}, u32[]{:S(2)}) %collective-permute-start.1) | collective-permute-done | bytes 878112 | tf_op jit(solution)/shard_map/ppermute | solution.py:30
  357.3 42.9 %concatenate.6 = bf16[2744,1280]{1,0:T(8,128)(2,1)} concatenate(bf16[343,1280]{1,0:T(8,128)(2,1)} %collective-permute-done.1, bf16[343,1280]{1,0:T(8,128)(2,1)} %collective-permute-done, bf16[343,1280]{1,0:T(8,128)(2,1)} %get-tuple-element.37, bf16[343,1280]{1,0:T(8,128)(2,1)} %collective-permute-done.2, bf16[343,1280]{1,0:T(8,128)(2,1)} %collective-permute-done.1, ...), dimensions={0} | concatenate | bytes 14049280 | tf_op jit(solution)/shard_map/jit(_roll_dynamic)/concatenate | solution.py:34
  403.2 6.6 convolution_multiply_fusion.2
  409.8 4.7 reshape.206
  417.8 4.8 convolution_add_fusion.1
  422.6 21.5 %multiply_convert_fusion = (bf16[1372,1280]{1,0:T(8,128)(2,1)}, f32[1372,1280]{1,0:T(8,128)}, f32[1372,1280]{1,0:T(8,128)}) fusion(f32[1372,1280]{1,0:T(8,128)S(1)} %convolution_add_fusion.1, f32[1372,16]{0,1:T(8,128)S(1)} %fusion.86, bf16[8,16,1280]{2,1,0:T(8,128)(2,1)} %param.47, s32[]{:T(128)S(6)} %select_n.98), kind=kOutput, calls=%fused_computation.21 | convolution fusion | flops 454845440 | bytes 24715012 | tf_op jit(solution)/shard_map/dot_general | solution.py:49
  444.1 12.8 %add_convert_fusion = bf16[1372,1280]{1,0:T(8,128)(2,1)} fusion(f32[1372,1280]{1,0:T(8,128)} %get-tuple-element.31, f32[1372,1280]{1,0:T(8,128)S(1)} %bitcast.182, bf16[1280,1280]{1,0:T(8,128)(2,1)} %param.40, f32[1372,1280]{1,0:T(8,128)} %get-tuple-element.47, bf16[2744,1280]{1,0:T(8,128)(2,1)} %concatenate.6, s32[]{:T(128)S(6)} %select_n.100), kind=kOutput, calls=%fused_computation.20 | convolution fusion | flops 4522112000 | bytes 31426564 | tf_op jit(solution)/shard_map/dot_general | solution.py:43
  460.1 4.8 fusion.159
  464.9 6.0 fusion.10
  470.9 36.2 %fusion.2 = bf16[344,1280]{1,0:T(8,128)(2,1)} fusion(bf16[1372,1280]{1,0:T(8,128)(2,1)} %fusion.10), kind=kCustom, calls=%all-reduce-scatter.2 | all-reduce-scatter fusion | flops 1761281 | bytes 4393472
  510.1 6.8 concatenate.9
  530.1 4.5 fusion.37
  541.0 4.8 fusion.158
  545.8 6.5 fusion.11
  552.3 6.7 all-gather.11.cloned.1.call-done
  559.0 4.7 reshape.208
  585.2 5.1 fusion.62
  600.3 5.2 copy.117
  625.0 4.5 copy.116
  629.5 26.1 %reshape.202 = f32[7,4,14,14,14,14]{5,4,3,2,1,0:T(8,128)} reshape(f32[7,4,196,196]{3,2,1,0:T(8,128)} %copy.117) | data formatting | bytes 8605184 | tf_op jit(solution)/shard_map/reshape | solution.py:140
  655.6 19.9 %fusion.151 = (f32[7,4,14,14,14]{4,3,2,1,0:T(8,128)}, f32[7,4,14,14,14]{4,3,2,1,0:T(8,128)}) fusion(f32[7,4,14,14,14,14]{5,4,3,2,1,0:T(8,128)} %reshape.202), kind=kLoop, calls=%fused_computation.237 | loop fusion | flops 1997632 | bytes 4917248 | tf_op jit(solution)/shard_map/reduce_sum | solution.py:142
  707.8 6.4 convolution_bitcast_fusion
  714.2 5.7 fusion.9
  719.9 68.8 %fusion.152 = (bf16[344,1280]{1,0:T(8,128)(2,1)}, bf16[344,1280]{1,0:T(8,128)(2,1)}) fusion(bf16[1372,1280]{1,0:T(8,128)(2,1)} %fusion.11, bf16[1372,1280]{1,0:T(8,128)(2,1)} %fusion.9), kind=kCustom, calls=%all-reduce-scatter.4 | all-reduce-scatter fusion | flops 3522561 | bytes 8786432
  794.6 6.0 concatenate.10
  800.7 6.0 concatenate.8
  809.0 5.6 fusion.52
  814.6 31.3 %all-reduce.14.cloned.1.call-done = (f32[8,1280,16]{1,2,0:T(8,128)}, f32[8,16,1280]{2,1,0:T(8,128)}, f32[8,1280,16]{1,2,0:T(8,128)}, f32[8,16,1280]{2,1,0:T(8,128)}) async-done(((f32[8,1280,16]{1,2,0:T(8,128)}, f32[8,16,1280]{2,1,0:T(8,128)}, f32[8,1280,16]{1,2,0:T(8,128)}, f32[8,16,1280]{2,1,0:T(8,128)}), (f32[8,1280,16]{1,2,0:T(8,128)}, f32[8,16,1280]{2,1,0:T(8,128)}, f32[8,1280,16]{1,2,0:T(8,128)}, ...) | async-done | bytes 2621456 | tf_op jit(solution)/shard_map/psum | solution.py:341
  845.9 107.7 %all-reduce.16.cloned.1.call-done = (f32[8,16,3,320]{3,1,2,0:T(8,128)}, f32[8,320,16]{1,2,0:T(8,128)}, f32[8,16,1280]{2,1,0:T(8,128)}, f32[8,1280,16]{1,2,0:T(8,128)}) async-done(((f32[8,16,3,320]{3,1,2,0:T(8,128)}, f32[8,320,16]{1,2,0:T(8,128)}, f32[8,16,1280]{2,1,0:T(8,128)}, f32[8,1280,16]{1,2,0:T(8,128)}), (f32[8,16,3,320]{3,1,2,0:T(8,128)}, f32[8,320,16]{1,2,0:T(8,128)}, f32[8,16,1280]{2,1,0:T(8,128)}, ...) | async-done | bytes 1966096 | tf_op jit(solution)/shard_map/psum | solution.py:332
  (289 shorter events, 213.5 us)
Async XLA Ops:
  7.2 410.5 %copy-start = (bf16[1280,1280]{1,0:T(8,128)(2,1)S(1)}, bf16[1280,1280]{1,0:T(8,128)(2,1)}, u32[]{:S(2)}) copy-start(bf16[1280,1280]{1,0:T(8,128)(2,1)} %param.38) | copy-start | bytes 9830404
  7.2 7.4 copy-start.68
  7.2 9.3 copy-start.63
  7.2 11.0 %copy-start.66 = (bf16[27,80]{1,0:T(8,128)(2,1)S(1)}, bf16[27,80]{1,0:T(8,128)(2,1)}, u32[]{:S(2)}) copy-start(bf16[27,80]{1,0:T(8,128)(2,1)} %param.33) | copy-start | bytes 12964
  7.2 11.4 %copy-start.67 = (bf16[27,80]{1,0:T(8,128)(2,1)S(1)}, bf16[27,80]{1,0:T(8,128)(2,1)}, u32[]{:S(2)}) copy-start(bf16[27,80]{1,0:T(8,128)(2,1)} %param.32) | copy-start | bytes 12964
  7.2 40.8 %all-gather.7.cloned.1.call-start = ((), (), s32[]{:S(2)}) async-start(), calls=%async_computation | async-start | bytes 4403200 | tf_op jit(solution)/shard_map/all_gather | solution.py:224
  8.8 8.5 copy-start.52
  10.4 6.9 copy-start.55
  11.1 6.2 copy-start.47
  11.9 292.8 %copy-start.45 = (f32[343]{0:T(512)}, f32[343]{0:T(512)S(1)}, u32[]{:S(2)}) copy-start(f32[343]{0:T(512)S(1)} %fusion.148) | copy-start | bytes 4120
  14.6 395.3 %all-gather.9.cloned.1.call-start = ((), (), s32[]{:S(2)}) async-start(), calls=%async_computation.1 | async-start | bytes 4403200 | tf_op jit(solution)/shard_map/all_gather | solution.py:261
  18.3 43.5 %copy-start.42 = (bf16[16,960]{1,0:T(8,128)(2,1)}, bf16[16,960]{1,0:T(8,128)(2,1)S(1)}, u32[]{:S(2)}) copy-start(bf16[16,960]{1,0:T(8,128)(2,1)S(1)} %reshape.189) | copy-start | bytes 92164
  18.7 93.9 %copy-start.37 = (bf16[14,14,80,1,1]{2,1,0,3,4:T(8,128)(2,1)}, bf16[14,14,80,1,1]{2,1,0,3,4:T(8,128)(2,1)S(1)}, u32[]{:S(2)}) copy-start(bf16[14,14,80,1,1]{2,1,0,3,4:T(8,128)(2,1)S(1)} %reshape.210) | copy-start | bytes 94084
  19.1 80.9 %copy-start.39 = (bf16[14,14,80,1,1]{2,1,0,3,4:T(8,128)(2,1)}, bf16[14,14,80,1,1]{2,1,0,3,4:T(8,128)(2,1)S(1)}, u32[]{:S(2)}) copy-start(bf16[14,14,80,1,1]{2,1,0,3,4:T(8,128)(2,1)S(1)} %reshape.209) | copy-start | bytes 94084
  55.9 5.8 copy-start.25
  255.3 37.5 %copy-start.58 = (bf16[1280]{0:T(1024)(128)(2,1)S(1)}, bf16[1280]{0:T(1024)(128)(2,1)}, u32[]{:S(2)}) copy-start(bf16[1280]{0:T(1024)(128)(2,1)} %param.35) | copy-start | bytes 7684
  255.3 37.6 %copy-start.59 = (bf16[1280]{0:T(1024)(128)(2,1)S(1)}, bf16[1280]{0:T(1024)(128)(2,1)}, u32[]{:S(2)}) copy-start(bf16[1280]{0:T(1024)(128)(2,1)} %param.36) | copy-start | bytes 7684
  255.3 37.6 %copy-start.60 = (bf16[1280]{0:T(1024)(128)(2,1)S(1)}, bf16[1280]{0:T(1024)(128)(2,1)}, u32[]{:S(2)}) copy-start(bf16[1280]{0:T(1024)(128)(2,1)} %param.37) | copy-start | bytes 7684
  255.3 37.6 %copy-start.64 = (u32[32]{0:T(128)S(1)}, u32[32]{0:T(128)}, u32[]{:S(2)}) copy-start(u32[32]{0:T(128)} %constant.229) | copy-start | bytes 388
  291.5 2.6 collective-permute-start.3
  292.8 13.8 %copy-start.49 = (f32[1280]{0:T(1024)}, f32[1280]{0:T(1024)S(1)}, u32[]{:S(2)}) copy-start(f32[1280]{0:T(1024)S(1)} %convert_element_type.173) | copy-start | bytes 15364
  302.4 39.1 %copy-start.61 = (bf16[1280]{0:T(1024)(128)(2,1)S(1)}, bf16[1280]{0:T(1024)(128)(2,1)}, u32[]{:S(2)}) copy-start(bf16[1280]{0:T(1024)(128)(2,1)} %param.39) | copy-start | bytes 7684
  304.7 52.6 %copy-start.54 = (f32[343]{0:T(512)}, f32[343]{0:T(512)S(1)}, u32[]{:S(2)}) copy-start(f32[343]{0:T(512)S(1)} %add_rsqrt_fusion) | copy-start | bytes 4120
  306.7 252.3 %all-gather.11.cloned.1.call-start = ((), (), s32[]{:S(2)}) async-start(), calls=%async_computation.2 | async-start | bytes 4403200 | tf_op jit(solution)/shard_map/all_gather | solution.py:308
  306.7 21.8 %collective-permute-start = (bf16[343,1280]{1,0:T(8,128)(2,1)}, bf16[343,1280]{1,0:T(8,128)(2,1)}, u32[]{:S(2)}, u32[]{:S(2)}) collective-permute-start(bf16[343,1280]{1,0:T(8,128)(2,1)} %get-tuple-element.37), channel_id=1, source_target_pairs={{0,1},{1,2},{2,3},{3,0},{4,5},{5,6},{6,7},{7,4},{8,9},{9,10},{10,1... | collective-permute-start | bytes 2634248 | tf_op jit(solution)/shard_map/ppermute | solution.py:30
  309.1 32.3 %collective-permute-start.2 = (bf16[343,1280]{1,0:T(8,128)(2,1)}, bf16[343,1280]{1,0:T(8,128)(2,1)}, u32[]{:S(2)}, u32[]{:S(2)}) collective-permute-start(bf16[343,1280]{1,0:T(8,128)(2,1)} %get-tuple-element.37), channel_id=1, source_target_pairs={{0,3},{1,0},{2,1},{3,2},{4,7},{5,4},{6,5},{7,6},{8,11},{9,8},{10,9... | collective-permute-start | bytes 2634248 | tf_op jit(solution)/shard_map/ppermute | solution.py:32
  328.5 28.7 %collective-permute-start.1 = (bf16[343,1280]{1,0:T(8,128)(2,1)}, bf16[343,1280]{1,0:T(8,128)(2,1)}, u32[]{:S(2)}, u32[]{:S(2)}) collective-permute-start(bf16[343,1280]{1,0:T(8,128)(2,1)} %collective-permute-done), channel_id=1, source_target_pairs={{0,1},{1,2},{2,3},{3,0},{4,5},{5,6},{6,7},{7,4},{8,9},{9,10},{10,1... | collective-permute-start | bytes 2634248 | tf_op jit(solution)/shard_map/ppermute | solution.py:30
  417.7 26.3 %slice-start.2 = ((s8[7045120]{0:T(1024)(128)(4,1)}), s8[4194304]{0:T(1024)(128)(4,1)S(1)}, s32[]{:S(2)}) async-start(s8[7045120]{0:T(1024)(128)(4,1)} %bitcast.181), calls=%async_computation.7 | async-start | bytes 8388608
  422.5 21.5 %slice-start.3 = ((s8[7045120]{0:T(1024)(128)(4,1)}), s8[2850816]{0:T(1024)(128)(4,1)S(1)}, s32[]{:S(2)}) async-start(s8[7045120]{0:T(1024)(128)(4,1)} %bitcast.181), calls=%async_computation.8 | async-start | bytes 5701632
  507.9 2.2 collective-permute-start.5
  524.2 321.7 %all-reduce.14.cloned.1.call-start = ((), (), s32[]{:S(2)}) async-start(), calls=%async_computation.3 | async-start | bytes 5242880 | tf_op jit(solution)/shard_map/psum | solution.py:341
  527.0 7.7 copy-start.12
  575.1 10.0 %copy-start.41 = (f32[7,4,196]{2,1,0:T(4,128)S(1)}, f32[7,4,196]{2,1,0:T(4,128)}, u32[]{:S(2)}) copy-start(f32[7,4,196]{2,1,0:T(4,128)} %log_add_fusion) | copy-start | bytes 65860
  585.2 9.4 slice-start
  655.6 19.9 %copy-start.38 = (bf16[14,14,80,1,1]{2,1,0,3,4:T(8,128)(2,1)S(1)}, bf16[14,14,80,1,1]{2,1,0,3,4:T(8,128)(2,1)}, u32[]{:S(2)}) copy-start(bf16[14,14,80,1,1]{2,1,0,3,4:T(8,128)(2,1)} %copy-done.37) | copy-start | bytes 94084
  698.8 7.3 copy-start.33
  707.5 246.1 %all-reduce.16.cloned.1.call-start = ((), (), s32[]{:S(2)}) async-start(), calls=%async_computation.4 | async-start | bytes 4194304 | tf_op jit(solution)/shard_map/psum | solution.py:332
  719.9 74.7 %copy-start.62 = (bf16[1280]{0:T(1024)(128)(2,1)S(1)}, bf16[1280]{0:T(1024)(128)(2,1)}, u32[]{:S(2)}) copy-start(bf16[1280]{0:T(1024)(128)(2,1)} %param.41) | copy-start | bytes 7684
  788.7 18.0 %copy-start.46 = (f32[343]{0:T(512)S(1)}, f32[343]{0:T(512)}, u32[]{:S(2)}) copy-start(f32[343]{0:T(512)} %copy-done.45) | copy-start | bytes 4120
  788.7 18.0 %copy-start.48 = (f32[1280]{0:T(1024)S(1)}, f32[1280]{0:T(1024)}, u32[]{:S(2)}) copy-start(f32[1280]{0:T(1024)} %copy-done.47) | copy-start | bytes 15364
  788.7 18.0 %copy-start.53 = (f32[343]{0:T(512)S(1)}, f32[343]{0:T(512)}, u32[]{:S(2)}) copy-start(f32[343]{0:T(512)} %copy-done.52) | copy-start | bytes 4120
  788.7 18.0 %copy-start.56 = (f32[343]{0:T(512)S(1)}, f32[343]{0:T(512)}, u32[]{:S(2)}) copy-start(f32[343]{0:T(512)} %copy-done.55) | copy-start | bytes 4120
  789.5 5.1 collective-permute-start.6
  791.5 9.2 collective-permute-start.4
  953.6 6.6 copy-start.29
  953.6 7.4 copy-start.32
  953.6 8.2 copy-start.31
  955.8 7.0 copy-start.28
  (37 other events, 129.4 us)
Sparse Core Ops, SparseCore 0:
  14.7 33.3 all-gather.6
  306.8 48.8 all-gather.8
  524.4 34.5 all-gather.10
  707.6 138.2 all-reduce.13
  851.4 102.1 all-reduce.15
